TPU v7x, 32 devices: a whole 2x2x4 slice. The times are simulated.
32 devices in a mesh: groups: 2 (over x), bricks: 16 (over z, y, core).
Axes of the slice: x: 2, y: 2, z: 4, core: 2. Of those that a mesh axis runs over, the one named last changes fastest.
Arguments:
- snapshots: bfloat16 [512, 32, 32, 256], P(('groups', 'bricks')), parts along dimension 0, may hold values from -30 to 30
- material: int32 [512, 1024], P(('groups', 'bricks')), parts along dimension 0, may hold values from 0 to 15
- occupancy: int32 [32, 4], P(('groups', 'bricks')), parts along dimension 0, may hold values 0 or 1
- moduli: bfloat16 [16], replicated, may hold values from 0.19921875 to 5
Outputs:
- energy_gram: float32 [512, 256], P(('groups', 'bricks')), parts along dimension 0
There are 2 independent parts, one for each index of `groups`. A program takes and returns all parts, laid end to end along the dimension named above; an argument that names none is the same for every part. Nothing has to cross between parts.
All inputs are finite; a program needn't handle non-finite values. No bound on the sum of `occupancy` on one device may be relied on, other than what follows from the above.
Results may differ from a plain program's by a relative error of at most 0.0003.
Values may be sent and summed in bfloat16 or wider, within the bound.
A program may use at most 128 MiB of HBM per device.

v0:
```python
import jax
import jax.numpy as jnp
from jax import lax
from jax.sharding import PartitionSpec as P


def with_halo(block, sides, width):
    for axis, dim in sides:
        count = lax.axis_size(axis)
        forward = [(i, i + 1) for i in range(count - 1)]
        backward = [(target, source) for source, target in forward]
        low = lax.ppermute(
            lax.slice_in_dim(block, block.shape[dim] - width, None, axis=dim), axis, forward
        )
        high = lax.ppermute(lax.slice_in_dim(block, 0, width, axis=dim), axis, backward)
        block = jnp.concatenate([low, block, high], axis=dim)
    return block


def stencil(padded_field, padded_modulus):
    depth = padded_field.shape[0] - 2
    rows_y = padded_field.shape[1]
    rows_x = padded_field.shape[2]
    field_full = jnp.pad(padded_field, ((0, 0), (1, 1), (1, 1), (0, 0)))
    modulus_full = jnp.pad(padded_modulus, ((0, 0), (1, 1), (1, 1)))
    center = field_full[1 : 1 + depth, 1 : 1 + rows_y, 1 : 1 + rows_x]
    center_mod = modulus_full[1 : 1 + depth, 1 : 1 + rows_y, 1 : 1 + rows_x]
    mod_sum = jnp.zeros_like(center_mod)
    field_sum = jnp.zeros_like(center)
    product_sum = jnp.zeros_like(center)
    total_weight = 0.0
    for shift_z in (-1, 0, 1):
        for shift_y in (-1, 0, 1):
            for shift_x in (-1, 0, 1):
                nonzero = abs(shift_z) + abs(shift_y) + abs(shift_x)
                if nonzero == 0:
                    continue
                weight = (1.0, 0.5, 0.25)[nonzero - 1]
                total_weight = total_weight + weight
                near = field_full[
                    1 + shift_z : 1 + shift_z + depth,
                    1 + shift_y : 1 + shift_y + rows_y,
                    1 + shift_x : 1 + shift_x + rows_x,
                ]
                near_mod = modulus_full[
                    1 + shift_z : 1 + shift_z + depth,
                    1 + shift_y : 1 + shift_y + rows_y,
                    1 + shift_x : 1 + shift_x + rows_x,
                ]
                mod_sum = mod_sum + weight * near_mod
                field_sum = field_sum + weight * near
                product_sum = product_sum + weight * near_mod[..., None] * near
    diagonal = 0.5 * (total_weight * center_mod + mod_sum)
    return (
        diagonal[..., None] * center - 0.5 * center_mod[..., None] * field_sum - 0.5 * product_sum
    )


def local(snapshots, material, occupancy, moduli):
    depth, rows_y, rows_x, width = snapshots.shape
    owners = lax.axis_size("bricks")
    tiles = occupancy.reshape(rows_y // 16, rows_x // 16)
    occupied = jnp.repeat(jnp.repeat(tiles, 16, 0), 16, 1).astype(jnp.bfloat16)
    classes = jnp.arange(moduli.shape[0], dtype=jnp.int32)
    matches = material[..., None] == classes
    looked = jnp.sum(jnp.where(matches, moduli.astype(jnp.float32), 0.0), axis=-1)
    modulus = looked.astype(jnp.bfloat16).reshape(depth, rows_y, rows_x) * occupied[None]
    field = snapshots * occupied[None, :, :, None]
    padded_field, padded_modulus = (
        with_halo(field, (("bricks", 0),), 1),
        with_halo(modulus, (("bricks", 0),), 1),
    )
    image = stencil(padded_field.astype(jnp.float32), padded_modulus.astype(jnp.float32)).astype(
        jnp.bfloat16
    )
    field_flat = field.reshape(-1, width)
    image_flat = image.reshape(-1, width)
    scale = 1.0 / (depth * rows_y * rows_x * owners)
    own_rows = width // owners
    local_gram = lax.dot_general(
        field_flat, image_flat, (((0,), (0,)), ((), ())), preferred_element_type=jnp.float32
    )
    summed = lax.psum(local_gram, "bricks")
    start = lax.axis_index("bricks") * own_rows
    result = lax.dynamic_slice_in_dim(summed, start, own_rows, 0)
    return result * scale


def solution(mesh):
    in_specs = (
        P(("groups", "bricks"), None, None, None),
        P(("groups", "bricks"), None),
        P(("groups", "bricks"), None),
        P(),
    )
    out_specs = P(("groups", "bricks"), None)
    return jax.shard_map(local, mesh=mesh, in_specs=in_specs, out_specs=out_specs, check_vma=False)
```

profile of v0, /device:TPU:0, one launch (start us, length us, event | category | flops | bytes accessed | tf_op | source)
XLA Modules:
  0.0 343.3 jit_solution(14337007187639578546)
XLA Ops:
  6.5 0.0 all-reduce.4.cloned.1.call-start
  6.5 0.7 convert_reduce_fusion
  7.2 0.1 convert_element_type.46
  7.3 0.1 copy.10
  7.4 0.1 broadcast_in_dim.12
  7.5 0.1 convert_element_type.47
  7.6 0.1 copy.11
  7.7 0.7 convert_element_type.49
  8.3 1.1 select_reduce_fusion
  9.5 0.1 convert_element_type.51
  9.7 2.4 collective-permute-start
  12.0 1.3 collective-permute-start.1
  13.3 8.0 %broadcast_multiply_fusion = bf16[16,32,32,256]{3,2,1,0:T(8,128)(2,1)} fusion(bf16[16,32,32,256]{3,2,1,0:T(8,128)(2,1)} %param.4, bf16[32,32]{1,0:T(8,128)(2,1)S(1)} %copy.11), kind=kLoop, calls=%fused_computation.30 | loop fusion | flops 4194304 | bytes 16779264 | tf_op jit(solution)/shard_map/mul | solution.py:68
  21.4 1.3 fusion.31
  22.6 5.2 %collective-permute-start.2 = (bf16[1,32,32,256]{3,2,1,0:T(8,128)(2,1)S(1)}, bf16[1,32,32,256]{3,2,1,0:T(8,128)(2,1)S(1)}, u32[]{:S(2)}, u32[]{:S(2)}) collective-permute-start(bf16[1,32,32,256]{3,2,1,0:T(8,128)(2,1)S(1)} %get-tuple-element.5), channel_id=1, source_target_pairs={{0,1},{1,2},{2,3},{3,4},{4,5},{5,6},{6,7},{7,8},{8,9},{9,10},{10,1... | collective-permute-start | bytes 1572872 | tf_op jit(solution)/shard_map/ppermute | solution.py:12
  27.8 1.3 collective-permute-start.3
  29.1 0.0 collective-permute-done
  29.1 0.0 collective-permute-done.1
  29.2 2.3 fusion.8
  31.5 3.5 %add_multiply_fusion = (f32[16,32,32]{2,1,0:T(8,128)S(1)}, f32[16,32,32]{2,1,0:T(8,128)S(1)}, f32[16,32,32]{2,1,0:T(8,128)S(1)}, f32[16,32,32]{2,1,0:T(8,128)S(1...) fusion(f32[18,32,32]{2,1,0:T(8,128)S(1)} %maximum_convert_fusion.1), kind=kLoop, calls=%fused_computation.78 | loop fusion | flops 966656 | bytes 2129920 | tf_op jit(solution)/shard_map/mul | solution.py:53
  35.1 0.0 collective-permute-done.2
  35.1 0.0 collective-permute-done.3
  35.1 11.4 %maximum_convert_fusion = f32[18,32,32,256]{3,2,1,0:T(8,128)} fusion(bf16[1,32,32,256]{3,2,1,0:T(8,128)(2,1)S(1)} %collective-permute-done.3, bf16[16,32,32,256]{3,2,1,0:T(8,128)(2,1)} %broadcast_multiply_fusion, bf16[1,32,32,256]{3,2,1,0:T(8,128)(2,1)S(1)} %collective-permute-done.2), kind=kLoop, calls=%fused_computation.28 | loop fusion | flops 14155776 | bytes 28311552 | tf_op jit(solution)/shard_map/convert_element_type | solution.py:73
  46.4 184.7 %fusion.37 = bf16[16,32,32,256]{3,2,1,0:T(8,128)(2,1)S(1)} fusion(f32[18,32,32,256]{3,2,1,0:T(8,128)} %maximum_convert_fusion, f32[16,32,32]{2,1,0:T(8,128)} %get-tuple-element.32, f32[16,32,32]{2,1,0:T(8,128)} %get-tuple-element.31, f32[16,32,32]{2,1,0:T(8,128)} %get-tuple-element.30, f32[16,32,32]{2,1,0:T(8,128)} %get-tuple-element.29, ...), kind=kLoop, calls=%fused_computation.27.clone.clone.clone.clone.1 | loop fusion | flops 427819008 | bytes 83951616 | tf_op jit(solution)/shard_map/dot_general | solution.py:80
  231.1 6.5 %fusion.5 = f32[256,256]{1,0:T(8,128)} fusion(bf16[16,32,32,256]{3,2,1,0:T(8,128)(2,1)} %broadcast_multiply_fusion, bf16[16,32,32,256]{3,2,1,0:T(8,128)(2,1)S(1)} %fusion.37), kind=kOutput, calls=%fused_computation.31 | convolution fusion | flops 2147483648 | bytes 17039360 | tf_op jit(solution)/shard_map/dot_general | solution.py:80
  237.6 0.0 all-reduce.4.cloned.1.call-update
  237.6 97.5 %all-reduce.4.cloned.1.call-done = f32[256,256]{1,0:T(8,128)} async-done(((f32[256,256]{1,0:T(8,128)}), f32[256,256]{1,0:T(8,128)}) %all-reduce.4.cloned.1.call-update) | async-done | bytes 262160 | tf_op jit(solution)/shard_map/psum | solution.py:83
  335.1 1.3 dynamic-slice_multiply_fusion
  (4 shorter events, 0.1 us)
Async XLA Ops:
  6.5 328.6 %all-reduce.4.cloned.1.call-start = ((), (), s32[]{:S(2)}) async-start(), calls=%async_computation | async-start | bytes 524288 | tf_op jit(solution)/shard_map/psum | solution.py:83
  9.7 19.5 %collective-permute-start = (bf16[1,32,32]{2,1,0:T(8,128)(2,1)S(1)}, bf16[1,32,32]{2,1,0:T(8,128)(2,1)S(1)}, u32[]{:S(2)}, u32[]{:S(2)}) collective-permute-start(bf16[1,32,32]{2,1,0:T(8,128)(2,1)S(1)} %get-tuple-element.35), channel_id=1, source_target_pairs={{0,1},{1,2},{2,3},{3,4},{4,5},{5,6},{6,7},{7,8},{8,9},{9,10},{10,1... | collective-permute-start | bytes 6152 | tf_op jit(solution)/shard_map/ppermute | solution.py:12
  12.0 17.1 %collective-permute-start.1 = (bf16[1,32,32]{2,1,0:T(8,128)(2,1)S(1)}, bf16[1,32,32]{2,1,0:T(8,128)(2,1)S(1)}, u32[]{:S(2)}, u32[]{:S(2)}) collective-permute-start(bf16[1,32,32]{2,1,0:T(8,128)(2,1)S(1)} %get-tuple-element.36), channel_id=1, source_target_pairs={{1,0},{2,1},{3,2},{4,3},{5,4},{6,5},{7,6},{8,7},{9,8},{10,9},{11,1... | collective-permute-start | bytes 6152 | tf_op jit(solution)/shard_map/ppermute | solution.py:15
  22.6 12.4 %collective-permute-start.2 = (bf16[1,32,32,256]{3,2,1,0:T(8,128)(2,1)S(1)}, bf16[1,32,32,256]{3,2,1,0:T(8,128)(2,1)S(1)}, u32[]{:S(2)}, u32[]{:S(2)}) collective-permute-start(bf16[1,32,32,256]{3,2,1,0:T(8,128)(2,1)S(1)} %get-tuple-element.5), channel_id=1, source_target_pairs={{0,1},{1,2},{2,3},{3,4},{4,5},{5,6},{6,7},{7,8},{8,9},{9,10},{10,1... | collective-permute-start | bytes 1572872 | tf_op jit(solution)/shard_map/ppermute | solution.py:12
  27.8 7.2 %collective-permute-start.3 = (bf16[1,32,32,256]{3,2,1,0:T(8,128)(2,1)S(1)}, bf16[1,32,32,256]{3,2,1,0:T(8,128)(2,1)S(1)}, u32[]{:S(2)}, u32[]{:S(2)}) collective-permute-start(bf16[1,32,32,256]{3,2,1,0:T(8,128)(2,1)S(1)} %get-tuple-element.6), channel_id=1, source_target_pairs={{1,0},{2,1},{3,2},{4,3},{5,4},{6,5},{7,6},{8,7},{9,8},{10,9},{11,1... | collective-permute-start | bytes 1572872 | tf_op jit(solution)/shard_map/ppermute | solution.py:15
Sparse Core Ops, SparseCore 0:
  237.8 97.3 all-reduce.3
where the time goes:
time: 344 us; the launch traced here: 343 us
  other arithmetic  214 us (62%)
  waiting for transfers between devices  97.5 us (28%)
  between operations  13.5 us (4%)
  starting transfers between devices  10.1 us (3%)
  matrix products  6.48 us (2%)
    dot_general x1, other arithmetic, local(): lax.dot_general(field_flat, image_flat, (((0,), (0,)), ((), ())), preferr...  185 us
    psum x1, waiting for transfers between devices, local(): summed = lax.psum(local_gram, 'bricks')  97.5 us
    convert_element_type x1, other arithmetic, local(): padded_field.astype(jnp.float32)  11.4 us
    mul x1, other arithmetic, local(): field = snapshots * occupied[None, :, :, None]  8.04 us
    ppermute x2, starting transfers between devices, with_halo(): lax.ppermute(lax.slice_in_dim(block, block.shape[dim] - width, None, axis...  7.56 us
  transfers between devices with their start and end apart: 5, of which 1 were waited for; matrix products, arithmetic and copies ran while one was open for 4% of the time, Pallas kernels for 0%

commit v1 on v0

v1 whole, which is shorter than its diff:
```python
import functools

import jax
import jax.numpy as jnp
from jax import lax
from jax.experimental import pallas as pl
from jax.experimental.pallas import tpu as pltpu
from jax.sharding import PartitionSpec as P


TRANSPOSED = (((0,), (0,)), ((), ()))


def windows(rows_y):
    found, first = [], 0
    start = 0
    while True:
        start = min(start, rows_y - 8)
        last = rows_y if start + 8 == rows_y else start + 7
        found.append((start, first, last))
        first = last
        if last == rows_y:
            return found
        start = last - 1


def fill_weights(ref, occupied, rows_y, rows_x):
    for start, first, last in windows(rows_y):
        shape = ((last - first) * rows_x, 8 * rows_x)
        row = lax.broadcasted_iota(jnp.int32, shape, 0)
        col = lax.broadcasted_iota(jnp.int32, shape, 1)
        gap_y = jnp.abs(row // rows_x + first - col // rows_x - start)
        gap_x = jnp.abs(row % rows_x - col % rows_x)
        weight = jnp.maximum(2 - gap_y, 0) * jnp.maximum(2 - gap_x, 0)
        here = occupied[:, start * rows_x : (start + 8) * rows_x]
        ref[first * rows_x : last * rows_x, :] = (weight.astype(jnp.float32) * here).astype(
            jnp.bfloat16
        )


def kernel(
    n, rows_y, rows_x, scale,
    snap, material, occupancy, moduli, out,
    field, ring, split, weights, weights_next, columns, total, share, arrived, edge_out, edge_in,
    load_sem, plane_send, plane_recv, edge_send, edge_recv, share_send, share_recv,
):
    me = lax.axis_index("bricks")
    depth, plane, width = snap.shape
    own = out.shape[0]

    loads = [
        pltpu.make_async_copy(snap.at[z], field.at[z], load_sem.at[z]) for z in range(depth)
    ]
    for load in loads:
        load.start()
    barrier = pltpu.get_barrier_semaphore()

    def greet(step, carry):
        pl.semaphore_signal(barrier, inc=1, device_id={"bricks": lax.rem(me + step, n)})
        return carry

    lax.fori_loop(1, n, greet, 0)

    place = lax.broadcasted_iota(jnp.int32, (1, plane), 1)
    at_x, at_y = place % rows_x, place // rows_x
    tile = (at_y // 16) * (rows_x // 16) + at_x // 16
    occupied = jnp.zeros((1, plane), jnp.float32)
    for t in range(occupancy.shape[1]):
        occupied = jnp.where(tile == t, occupancy[0, t].astype(jnp.float32), occupied)
    classes = material[...]
    modulus = jnp.zeros((depth, plane), jnp.float32)
    for c in range(moduli.shape[0]):
        modulus = jnp.where(classes == c, moduli[c], modulus)
    modulus = modulus * occupied
    edge_out[0, 0:1, :] = modulus[0:1]
    edge_out[0, 1:2, :] = occupied
    edge_out[0, 2:8, :] = jnp.zeros((6, plane), jnp.float32)
    edge_out[1, 0:1, :] = modulus[depth - 1 : depth]
    edge_out[1, 1:8, :] = jnp.zeros((7, plane), jnp.float32)

    below, above = lax.rem(me + n - 1, n), lax.rem(me + 1, n)

    def edge_copy(side):
        return pltpu.make_async_remote_copy(
            src_ref=edge_out.at[side],
            dst_ref=edge_in.at[side],
            send_sem=edge_send.at[side],
            recv_sem=edge_recv.at[side],
            device_id={"bricks": below if side == 0 else above},
        )

    def plane_copy():
        return pltpu.make_async_remote_copy(
            src_ref=snap.at[0],
            dst_ref=field.at[depth],
            send_sem=plane_send,
            recv_sem=plane_recv,
            device_id={"bricks": below},
        )

    pl.semaphore_wait(barrier, n - 1)

    @pl.when(me > 0)
    def _():
        edge_copy(0).start()
        plane_copy().start()

    @pl.when(me < n - 1)
    def _():
        edge_copy(1).start()

    @pl.when(me == n - 1)
    def _():
        edge_in[0] = jnp.zeros(edge_in.shape[1:], jnp.float32)
        field[depth] = jnp.zeros(field.shape[1:], jnp.bfloat16)

    @pl.when(me == 0)
    def _():
        edge_in[1] = jnp.zeros(edge_in.shape[1:], jnp.float32)

    fill_weights(weights, occupied, rows_y, rows_x)
    total[...] = jnp.zeros_like(total)
    ring[2] = jnp.zeros(ring.shape[1:], jnp.float32)

    @pl.when(me < n - 1)
    def _():
        edge_copy(0).wait_recv()

    @pl.when(me > 0)
    def _():
        edge_copy(1).wait_recv()

    fill_weights(weights_next, edge_in[0, 1:2, :], rows_y, rows_x)

    moduli_all = jnp.concatenate(
        [modulus, edge_in[0, 0:1, :], edge_in[1, 0:1, :], jnp.zeros((6, plane), jnp.float32)], 0
    )
    summed = moduli_all
    for at, count, step in ((at_x, rows_x, 1), (at_y, rows_y, rows_x)):
        lower = jnp.where(at > 0, pltpu.roll(summed, step, 1), 0.0)
        upper = jnp.where(at < count - 1, pltpu.roll(summed, plane - step, 1), 0.0)
        summed = lower + upper + 2.0 * summed
    around = (
        jnp.concatenate([summed[depth + 1 : depth + 2], summed[: depth - 1]], 0)
        + 2.0 * summed[:depth]
        + summed[1 : depth + 1]
    )
    diagonal = (4.0 * modulus + 0.0625 * around) * occupied
    diagonal_high = diagonal.astype(jnp.bfloat16).astype(jnp.float32)
    gap = jnp.zeros((32 - depth, plane), jnp.float32)
    stack = jnp.concatenate(
        [
            0.125 * moduli_all,
            jnp.zeros((8, plane), jnp.float32),
            diagonal_high,
            gap,
            diagonal - diagonal_high,
            gap,
            jnp.zeros((32, plane), jnp.float32),
        ],
        0,
    )
    columns[...] = stack.T.astype(jnp.bfloat16)

    def convolve(z, table, slot):
        for start, first, last in windows(rows_y):
            rows = slice(first * rows_x, last * rows_x)
            ring[slot, rows, :] = jnp.dot(
                table[rows, :],
                field[z, start * rows_x : (start + 8) * rows_x, :],
                preferred_element_type=jnp.float32,
            )

    def picker(z):
        row = lax.broadcasted_iota(jnp.int32, (128, 256), 0)
        col = lax.broadcasted_iota(jnp.int32, (128, 256), 1)
        is_modulus = (col < 128) & (row == z)
        is_diagonal = (col >= 128) & ((row == z + 32) | (row == z + 64))
        return jnp.where(is_modulus | is_diagonal, 1.0, 0.0).astype(jnp.bfloat16)

    def put(rows, part, value):
        high = value.astype(jnp.bfloat16)
        split[rows, part * 128 : (part + 1) * 128] = high
        split[rows, width + part * 128 : width + (part + 1) * 128] = (
            value - high.astype(jnp.float32)
        ).astype(jnp.bfloat16)

    def add_gram(z):
        total[...] += lax.dot_general(
            field[z], split[...], TRANSPOSED, preferred_element_type=jnp.float32
        )

    def one_plane(z, table):
        older, now, newer = lax.rem(z + 2, 3), lax.rem(z, 3), lax.rem(z + 1, 3)
        pick = picker(z)
        for start, first, last in windows(rows_y):
            rows = slice(first * rows_x, last * rows_x)
            fresh = jnp.dot(
                table[rows, :],
                field[z + 1, start * rows_x : (start + 8) * rows_x, :],
                preferred_element_type=jnp.float32,
            )
            ring[newer, rows, :] = fresh
            spread = jnp.dot(columns[rows, :], pick, preferred_element_type=jnp.float32)
            for part in range(width // 128):
                lanes = slice(part * 128, (part + 1) * 128)
                around = ring[older, rows, lanes] + 2.0 * ring[now, rows, lanes] + fresh[:, lanes]
                value = (
                    spread[:, 128:] * field[z, rows, lanes].astype(jnp.float32)
                    - spread[:, :128] * around
                )
                put(rows, part, value)
        add_gram(z)

    loads[0].wait()
    convolve(0, weights, 0)

    def step(z, carry):
        pltpu.make_async_copy(snap.at[z + 1], field.at[z + 1], load_sem.at[z + 1]).wait()
        one_plane(z, weights)
        return carry

    lax.fori_loop(0, depth - 1, step, 0)

    @pl.when(me < n - 1)
    def _():
        plane_copy().wait_recv()

    one_plane(depth - 1, weights_next)
    pick = picker(depth)
    for start, first, last in windows(rows_y):
        rows = slice(first * rows_x, last * rows_x)
        spread = jnp.dot(columns[rows, :], pick, preferred_element_type=jnp.float32)
        for part in range(width // 128):
            lanes = slice(part * 128, (part + 1) * 128)
            put(rows, part, -spread[:, :128] * ring[(depth - 1) % 3, rows, lanes])
    add_gram(depth)

    half = total[:, :width] + total[:, width:]
    gram = (half + half.T) * scale
    for j in range(n):
        share[j] = gram[j * own : (j + 1) * own, :]

    def share_copy(step):
        peer = lax.rem(me + step, n)
        return pltpu.make_async_remote_copy(
            src_ref=share.at[peer],
            dst_ref=arrived.at[step],
            send_sem=share_send.at[step],
            recv_sem=share_recv.at[step],
            device_id={"bricks": peer},
        )

    def send(step, carry):
        share_copy(step).start()
        return carry

    lax.fori_loop(1, n, send, 0)

    def receive(step, result):
        share_copy(step).wait_recv()
        return result + arrived[step]

    out[...] = lax.fori_loop(1, n, receive, share[me])

    def finish(step, carry):
        share_copy(step).wait_send()
        return carry

    lax.fori_loop(1, n, finish, 0)

    @pl.when(me > 0)
    def _():
        edge_copy(0).wait_send()
        plane_copy().wait_send()

    @pl.when(me < n - 1)
    def _():
        edge_copy(1).wait_send()


def local(snapshots, material, occupancy, moduli):
    depth, rows_y, rows_x, width = snapshots.shape
    plane = rows_y * rows_x
    n = lax.axis_size("bricks")
    own = width // n
    f32, bf16 = jnp.float32, jnp.bfloat16
    vmem = pl.BlockSpec(memory_space=pltpu.VMEM)
    smem = pl.BlockSpec(memory_space=pltpu.SMEM)
    flops = 2 * depth * plane * 256 * (2 * width + 3 * 256)
    return pl.pallas_call(
        functools.partial(kernel, n, rows_y, rows_x, 1.0 / (depth * plane * n)),
        out_shape=jax.ShapeDtypeStruct((own, width), f32),
        in_specs=[pl.BlockSpec(memory_space=pl.ANY), vmem, smem, smem],
        out_specs=vmem,
        scratch_shapes=[
            pltpu.VMEM((depth + 1, plane, width), bf16),
            pltpu.VMEM((3, plane, width), f32),
            pltpu.VMEM((plane, 2 * width), bf16),
            pltpu.VMEM((plane, 8 * rows_x), bf16),
            pltpu.VMEM((plane, 8 * rows_x), bf16),
            pltpu.VMEM((plane, 128), bf16),
            pltpu.VMEM((width, 2 * width), f32),
            pltpu.VMEM((n, own, width), f32),
            pltpu.VMEM((n, own, width), f32),
            pltpu.VMEM((2, 8, plane), f32),
            pltpu.VMEM((2, 8, plane), f32),
            pltpu.SemaphoreType.DMA((depth,)),
            pltpu.SemaphoreType.DMA,
            pltpu.SemaphoreType.DMA,
            pltpu.SemaphoreType.DMA((2,)),
            pltpu.SemaphoreType.DMA((2,)),
            pltpu.SemaphoreType.DMA((n,)),
            pltpu.SemaphoreType.DMA((n,)),
        ],
        compiler_params=pltpu.CompilerParams(
            collective_id=0, has_side_effects=True, vmem_limit_bytes=48 * 1024 * 1024
        ),
        cost_estimate=pl.CostEstimate(
            flops=flops, bytes_accessed=depth * plane * width * 2, transcendentals=0
        ),
    )(
        snapshots.reshape(depth, plane, width),
        material,
        occupancy,
        moduli.astype(f32),
    )


def solution(mesh):
    in_specs = (
        P(("groups", "bricks"), None, None, None),
        P(("groups", "bricks"), None),
        P(("groups", "bricks"), None),
        P(),
    )
    out_specs = P(("groups", "bricks"), None)
    return jax.shard_map(local, mesh=mesh, in_specs=in_specs, out_specs=out_specs, check_vma=False)
```

time: 344 us -> 36.3 us (0.11)
  other arithmetic: 214 us -> 0.66 us
  waiting for transfers between devices: 97.5 us -> 0 us
  Pallas kernels: 0 us -> 33.2 us
  between operations: 13.5 us -> 0.01 us
  starting transfers between devices: 10.1 us -> 0 us
  matrix products: 6.48 us -> 0 us
    dot_general x1 -> x0, other arithmetic: 185 us -> none  [local(): lax.dot_general(field_flat, image_flat, (((0,), (0,)), ((), ())), preferr...]
    psum x1 -> x0, waiting for transfers between devices: 97.5 us -> none  [local(): summed = lax.psum(local_gram, 'bricks')]
    pallas_call x0 -> x1, Pallas kernels: none -> 33.2 us  [local(): pl.pallas_call(functools.partial(kernel, n, rows_y, rows_x, 1.0 / (depth...]
    mul x5 -> x0, other arithmetic: 15.2 us -> none  [the longest x1 8.04 us: local(): field = snapshots * occupied[None, :, :, None]]
    convert_element_type x4 -> x1, other arithmetic: 12.7 us -> 0.66 us  [local(): moduli.astype(f32)]
    ppermute x4 -> x0, starting transfers between devices: 10.1 us -> none  [the longest x2 7.56 us: with_halo(): lax.ppermute(lax.slice_in_dim(block, block.shape[dim] - width, None, axis...]
    dot_general x1 -> x0, matrix products: 6.48 us -> none  [local(): lax.dot_general(field_flat, image_flat, (((0,), (0,)), ((), ())), preferr...]
  transfers between devices with their start and end apart: 5 -> 0, of which waited for: 1 -> 0; matrix products, arithmetic and copies ran while one was open for 4% -> 0% of each run, Pallas kernels for 0% -> 0%
where the time goes in v1:
time: 36.3 us; the launch traced here: 36 us
  Pallas kernels  33.2 us (91%)
  local copies, waits for them, and re-layouts  2.1 us (6%)
  other arithmetic  0.66 us (2%)
    pallas_call x1, Pallas kernels, local(): pl.pallas_call(functools.partial(kernel, n, rows_y, rows_x, 1.0 / (depth...  33.2 us
    unnamed x5, local copies, waits for them, and re-layouts  2.1 us

profile of v1, /device:TPU:0, one launch (start us, length us, event | category | flops | bytes accessed | tf_op | source)
XLA Modules:
  0.0 36.0 jit_solution(940811671445642888)
XLA Ops:
  0.0 0.7 %convert_element_type.3.moduli = f32[16]{0:T(128)S(1)} convert(bf16[16]{0:T(256)(128)(2,1)} %param.7) | non-fusion elementwise | flops 16 | bytes 96 | tf_op jit(solution)/shard_map/convert_element_type | solution.py:326
  0.7 0.0 copy-start
  0.7 0.8 %copy-done = s32[16,1024]{1,0:T(8,128)S(1)} copy-done((s32[16,1024]{1,0:T(8,128)S(1)}, s32[16,1024]{1,0:T(8,128)}, u32[]{:S(2)}) %copy-start) | copy-done | bytes 65560
  1.5 0.0 copy-start.1
  1.5 0.7 %copy-done.1 = s32[1,4]{1,0:T(1,128)S(1)} copy-done((s32[1,4]{1,0:T(1,128)S(1)}, s32[1,4]{1,0:T(1,128)}, u32[]{:S(2)}) %copy-start.1) | copy-done | bytes 40
  2.2 33.2 %shard_map.46 = f32[16,256]{1,0:T(8,128)S(1)} custom-call(bf16[16,1024,256]{2,1,0:T(8,128)(2,1)} %bitcast.1, s32[16,1024]{1,0:T(8,128)S(1)} %copy-done, s32[1,4]{1,0:T(1,128)S(1)} %copy-done.1, f32[16]{0:T(128)S(1)} %convert_element_type.3.moduli), custom_call_target="tpu_custom_call" | custom-call | flops 10737418240 | bytes 8388608 | tf_op jit(solution)/shard_map/pallas_call | solution.py:291
  35.4 0.6 %copy.6 = f32[16,256]{1,0:T(8,128)} copy(f32[16,256]{1,0:T(8,128)S(1)} %shard_map.46) | data formatting | bytes 32768
Async XLA Ops:
  0.7 0.8 %copy-start = (s32[16,1024]{1,0:T(8,128)S(1)}, s32[16,1024]{1,0:T(8,128)}, u32[]{:S(2)}) copy-start(s32[16,1024]{1,0:T(8,128)} %material.1) | copy-start | bytes 196612
  1.5 0.7 %copy-start.1 = (s32[1,4]{1,0:T(1,128)S(1)}, s32[1,4]{1,0:T(1,128)}, u32[]{:S(2)}) copy-start(s32[1,4]{1,0:T(1,128)} %occupancy.1) | copy-start | bytes 52

commit v2 on v1

--- a/solution.py
+++ b/solution.py
@@ -40,9 +40,11 @@
 
 def kernel(
     n, rows_y, rows_x, scale,
-    snap, material, occupancy, moduli, out,
-    field, ring, split, weights, weights_next, columns, total, share, arrived, edge_out, edge_in,
-    load_sem, plane_send, plane_recv, edge_send, edge_recv, share_send, share_recv,
+    snap, material_in, occupancy_in, moduli_in, out,
+    field, newest, pair, split, weights, weights_next, columns, total, share, mate, mine, arrived,
+    edge_out, edge_in, material, occupancy, moduli,
+    load_sem, small_sem, plane_send, plane_recv, edge_send, edge_recv, share_send, share_recv,
+    mate_send, mate_recv,
 ):
     me = lax.axis_index("bricks")
     depth, plane, width = snap.shape
@@ -51,34 +53,45 @@
     loads = [
         pltpu.make_async_copy(snap.at[z], field.at[z], load_sem.at[z]) for z in range(depth)
     ]
-    for load in loads:
+    small = [
+        pltpu.make_async_copy(source, target, small_sem.at[i])
+        for i, (source, target) in enumerate(
+            ((material_in, material), (occupancy_in, occupancy), (moduli_in, moduli))
+        )
+    ]
+    for load in small + loads:
         load.start()
     barrier = pltpu.get_barrier_semaphore()
+    below, above = lax.rem(me + n - 1, n), lax.rem(me + 1, n)
+    core = lax.rem(me, 2)
+    other_core = me + 1 - 2 * core
+    for neighbour in (below, above):
+        pl.semaphore_signal(barrier, inc=1, device_id={"bricks": neighbour})
 
     def greet(step, carry):
-        pl.semaphore_signal(barrier, inc=1, device_id={"bricks": lax.rem(me + step, n)})
+        pl.semaphore_signal(barrier, inc=1, device_id={"bricks": lax.rem(me + 2 * step, n)})
         return carry
 
-    lax.fori_loop(1, n, greet, 0)
+    lax.fori_loop(1, n // 2, greet, 0)
+    for load in small:
+        load.wait()
 
     place = lax.broadcasted_iota(jnp.int32, (1, plane), 1)
     at_x, at_y = place % rows_x, place // rows_x
     tile = (at_y // 16) * (rows_x // 16) + at_x // 16
     occupied = jnp.zeros((1, plane), jnp.float32)
     for t in range(occupancy.shape[1]):
-        occupied = jnp.where(tile == t, occupancy[0, t].astype(jnp.float32), occupied)
+        occupied = jnp.where(tile == t, occupancy[0:1, t : t + 1].astype(jnp.float32), occupied)
     classes = material[...]
     modulus = jnp.zeros((depth, plane), jnp.float32)
-    for c in range(moduli.shape[0]):
-        modulus = jnp.where(classes == c, moduli[c], modulus)
+    for c in range(moduli.shape[1]):
+        modulus = jnp.where(classes == c, moduli[0:1, c : c + 1], modulus)
     modulus = modulus * occupied
     edge_out[0, 0:1, :] = modulus[0:1]
     edge_out[0, 1:2, :] = occupied
     edge_out[0, 2:8, :] = jnp.zeros((6, plane), jnp.float32)
     edge_out[1, 0:1, :] = modulus[depth - 1 : depth]
     edge_out[1, 1:8, :] = jnp.zeros((7, plane), jnp.float32)
-
-    below, above = lax.rem(me + n - 1, n), lax.rem(me + 1, n)
 
     def edge_copy(side):
         return pltpu.make_async_remote_copy(
@@ -98,7 +111,7 @@
             device_id={"bricks": below},
         )
 
-    pl.semaphore_wait(barrier, n - 1)
+    pl.semaphore_wait(barrier, n // 2 + 1)
 
     @pl.when(me > 0)
     def _():
@@ -120,7 +133,17 @@
 
     fill_weights(weights, occupied, rows_y, rows_x)
     total[...] = jnp.zeros_like(total)
-    ring[2] = jnp.zeros(ring.shape[1:], jnp.float32)
+    split[1] = jnp.zeros(split.shape[1:], jnp.bfloat16)
+    loads[0].wait()
+    for start, first, last in windows(rows_y):
+        rows = slice(first * rows_x, last * rows_x)
+        fresh = jnp.dot(
+            weights[rows, :],
+            field[0, start * rows_x : (start + 8) * rows_x, :],
+            preferred_element_type=jnp.float32,
+        )
+        newest[rows, :] = fresh
+        pair[rows, :] = fresh
 
     @pl.when(me < n - 1)
     def _():
@@ -162,15 +185,6 @@
     )
     columns[...] = stack.T.astype(jnp.bfloat16)
 
-    def convolve(z, table, slot):
-        for start, first, last in windows(rows_y):
-            rows = slice(first * rows_x, last * rows_x)
-            ring[slot, rows, :] = jnp.dot(
-                table[rows, :],
-                field[z, start * rows_x : (start + 8) * rows_x, :],
-                preferred_element_type=jnp.float32,
-            )
-
     def picker(z):
         row = lax.broadcasted_iota(jnp.int32, (128, 256), 0)
         col = lax.broadcasted_iota(jnp.int32, (128, 256), 1)
@@ -178,73 +192,92 @@
         is_diagonal = (col >= 128) & ((row == z + 32) | (row == z + 64))
         return jnp.where(is_modulus | is_diagonal, 1.0, 0.0).astype(jnp.bfloat16)
 
-    def put(rows, part, value):
+    def put(slot, rows, part, value):
         high = value.astype(jnp.bfloat16)
-        split[rows, part * 128 : (part + 1) * 128] = high
-        split[rows, width + part * 128 : width + (part + 1) * 128] = (
+        split[slot, rows, part * 128 : (part + 1) * 128] = high
+        split[slot, rows, width + part * 128 : width + (part + 1) * 128] = (
             value - high.astype(jnp.float32)
         ).astype(jnp.bfloat16)
 
-    def add_gram(z):
+    def add_gram(z, slot):
         total[...] += lax.dot_general(
-            field[z], split[...], TRANSPOSED, preferred_element_type=jnp.float32
-        )
-
-    def one_plane(z, table):
-        older, now, newer = lax.rem(z + 2, 3), lax.rem(z, 3), lax.rem(z + 1, 3)
+            field[z], split[slot], TRANSPOSED, preferred_element_type=jnp.float32
+        )
+
+    def one_plane(z, slot, table, last_plane=False):
         pick = picker(z)
-        for start, first, last in windows(rows_y):
+        for index, (start, first, last) in enumerate(windows(rows_y)):
             rows = slice(first * rows_x, last * rows_x)
             fresh = jnp.dot(
                 table[rows, :],
                 field[z + 1, start * rows_x : (start + 8) * rows_x, :],
                 preferred_element_type=jnp.float32,
             )
-            ring[newer, rows, :] = fresh
             spread = jnp.dot(columns[rows, :], pick, preferred_element_type=jnp.float32)
             for part in range(width // 128):
                 lanes = slice(part * 128, (part + 1) * 128)
-                around = ring[older, rows, lanes] + 2.0 * ring[now, rows, lanes] + fresh[:, lanes]
+                later = newest[rows, lanes] + fresh[:, lanes]
+                around = pair[rows, lanes] + later
+                if not last_plane:
+                    newest[rows, lanes] = fresh[:, lanes]
+                    pair[rows, lanes] = later
                 value = (
                     spread[:, 128:] * field[z, rows, lanes].astype(jnp.float32)
                     - spread[:, :128] * around
                 )
-                put(rows, part, value)
-        add_gram(z)
-
-    loads[0].wait()
-    convolve(0, weights, 0)
-
-    def step(z, carry):
-        pltpu.make_async_copy(snap.at[z + 1], field.at[z + 1], load_sem.at[z + 1]).wait()
-        one_plane(z, weights)
+                put(slot, rows, part, value)
+            if index == 2:
+                add_gram(jnp.maximum(z - 1, 0), 1 - slot)
+
+    def wait_plane(z):
+        pltpu.make_async_copy(snap.at[z], field.at[z], load_sem.at[z]).wait()
+
+    def step(i, carry):
+        wait_plane(2 * i + 1)
+        wait_plane(2 * i + 2)
+        one_plane(2 * i, 0, weights)
+        one_plane(2 * i + 1, 1, weights)
         return carry
 
-    lax.fori_loop(0, depth - 1, step, 0)
+    lax.fori_loop(0, depth // 2 - 1, step, 0)
+    wait_plane(depth - 1)
+    one_plane(depth - 2, 0, weights)
 
     @pl.when(me < n - 1)
     def _():
         plane_copy().wait_recv()
 
-    one_plane(depth - 1, weights_next)
+    one_plane(depth - 1, 1, weights_next, last_plane=True)
     pick = picker(depth)
     for start, first, last in windows(rows_y):
         rows = slice(first * rows_x, last * rows_x)
         spread = jnp.dot(columns[rows, :], pick, preferred_element_type=jnp.float32)
         for part in range(width // 128):
             lanes = slice(part * 128, (part + 1) * 128)
-            put(rows, part, -spread[:, :128] * ring[(depth - 1) % 3, rows, lanes])
-    add_gram(depth)
+            put(0, rows, part, -spread[:, :128] * newest[rows, lanes])
+    add_gram(depth - 1, 1)
+    add_gram(depth, 0)
 
     half = total[:, :width] + total[:, width:]
     gram = (half + half.T) * scale
     for j in range(n):
-        share[j] = gram[j * own : (j + 1) * own, :]
+        share[j % 2, j // 2] = gram[j * own : (j + 1) * own, :]
+
+    mate_copy = pltpu.make_async_remote_copy(
+        src_ref=share.at[1 - core],
+        dst_ref=mate,
+        send_sem=mate_send,
+        recv_sem=mate_recv,
+        device_id={"bricks": other_core},
+    )
+    mate_copy.start()
+    mate_copy.wait_recv()
+    mine[...] = share[core] + mate[...]
 
     def share_copy(step):
-        peer = lax.rem(me + step, n)
+        peer = lax.rem(me + 2 * step, n)
         return pltpu.make_async_remote_copy(
-            src_ref=share.at[peer],
+            src_ref=mine.at[peer // 2],
             dst_ref=arrived.at[step],
             send_sem=share_send.at[step],
             recv_sem=share_recv.at[step],
@@ -255,19 +288,20 @@
         share_copy(step).start()
         return carry
 
-    lax.fori_loop(1, n, send, 0)
+    lax.fori_loop(1, n // 2, send, 0)
 
     def receive(step, result):
         share_copy(step).wait_recv()
         return result + arrived[step]
 
-    out[...] = lax.fori_loop(1, n, receive, share[me])
+    out[...] = lax.fori_loop(1, n // 2, receive, mine[me // 2])
 
     def finish(step, carry):
         share_copy(step).wait_send()
         return carry
 
-    lax.fori_loop(1, n, finish, 0)
+    lax.fori_loop(1, n // 2, finish, 0)
+    mate_copy.wait_send()
 
     @pl.when(me > 0)
     def _():
@@ -286,35 +320,43 @@
     own = width // n
     f32, bf16 = jnp.float32, jnp.bfloat16
     vmem = pl.BlockSpec(memory_space=pltpu.VMEM)
-    smem = pl.BlockSpec(memory_space=pltpu.SMEM)
     flops = 2 * depth * plane * 256 * (2 * width + 3 * 256)
     return pl.pallas_call(
         functools.partial(kernel, n, rows_y, rows_x, 1.0 / (depth * plane * n)),
         out_shape=jax.ShapeDtypeStruct((own, width), f32),
-        in_specs=[pl.BlockSpec(memory_space=pl.ANY), vmem, smem, smem],
+        in_specs=[pl.BlockSpec(memory_space=pl.ANY)] * 4,
         out_specs=vmem,
         scratch_shapes=[
             pltpu.VMEM((depth + 1, plane, width), bf16),
-            pltpu.VMEM((3, plane, width), f32),
-            pltpu.VMEM((plane, 2 * width), bf16),
+            pltpu.VMEM((plane, width), f32),
+            pltpu.VMEM((plane, width), f32),
+            pltpu.VMEM((2, plane, 2 * width), bf16),
             pltpu.VMEM((plane, 8 * rows_x), bf16),
             pltpu.VMEM((plane, 8 * rows_x), bf16),
             pltpu.VMEM((plane, 128), bf16),
             pltpu.VMEM((width, 2 * width), f32),
-            pltpu.VMEM((n, own, width), f32),
-            pltpu.VMEM((n, own, width), f32),
+            pltpu.VMEM((2, n // 2, own, width), f32),
+            pltpu.VMEM((n // 2, own, width), f32),
+            pltpu.VMEM((n // 2, own, width), f32),
+            pltpu.VMEM((n // 2, own, width), f32),
             pltpu.VMEM((2, 8, plane), f32),
             pltpu.VMEM((2, 8, plane), f32),
+            pltpu.VMEM(material.shape, jnp.int32),
+            pltpu.VMEM(occupancy.shape, jnp.int32),
+            pltpu.VMEM((1, moduli.shape[0]), f32),
             pltpu.SemaphoreType.DMA((depth,)),
+            pltpu.SemaphoreType.DMA((3,)),
             pltpu.SemaphoreType.DMA,
             pltpu.SemaphoreType.DMA,
             pltpu.SemaphoreType.DMA((2,)),
             pltpu.SemaphoreType.DMA((2,)),
-            pltpu.SemaphoreType.DMA((n,)),
-            pltpu.SemaphoreType.DMA((n,)),
+            pltpu.SemaphoreType.DMA((n // 2,)),
+            pltpu.SemaphoreType.DMA((n // 2,)),
+            pltpu.SemaphoreType.DMA,
+            pltpu.SemaphoreType.DMA,
         ],
         compiler_params=pltpu.CompilerParams(
-            collective_id=0, has_side_effects=True, vmem_limit_bytes=48 * 1024 * 1024
+            collective_id=0, has_side_effects=True, vmem_limit_bytes=64 * 1024 * 1024
         ),
         cost_estimate=pl.CostEstimate(
             flops=flops, bytes_accessed=depth * plane * width * 2, transcendentals=0
@@ -323,7 +365,7 @@
         snapshots.reshape(depth, plane, width),
         material,
         occupancy,
-        moduli.astype(f32),
+        moduli.astype(f32).reshape(1, -1),
     )
 
 

time: 36.3 us -> 32 us (0.88)
  Pallas kernels: 33.2 us -> 29.3 us
  local copies, waits for them, and re-layouts: 2.1 us -> 1.32 us
  other arithmetic: 0.66 us -> 1.17 us
    pallas_call x1, Pallas kernels: 33.2 us -> 29.3 us  [local(): pl.pallas_call(functools.partial(kernel, n, rows_y, rows_x, 1.0 / (depth...]
    reshape x0 -> x1, other arithmetic: none -> 1.17 us  [local(): moduli.astype(f32).reshape(1, -1)]
    unnamed x5 -> x1, local copies, waits for them, and re-layouts: 2.1 us -> 1.32 us
    convert_element_type x1 -> x0, other arithmetic: 0.66 us -> none  [local(): moduli.astype(f32)]
where the time goes in v2:
time: 32 us; the launch traced here: 31.8 us
  Pallas kernels  29.3 us (92%)
  local copies, waits for them, and re-layouts  1.32 us (4%)
  other arithmetic  1.17 us (4%)
    pallas_call x1, Pallas kernels, local(): pl.pallas_call(functools.partial(kernel, n, rows_y, rows_x, 1.0 / (depth...  29.3 us
    unnamed x1, local copies, waits for them, and re-layouts  1.32 us
    reshape x1, other arithmetic, local(): moduli.astype(f32).reshape(1, -1)  1.17 us

profile of v2, /device:TPU:0, one launch (start us, length us, event | category | flops | bytes accessed | tf_op | source)
XLA Modules:
  0.0 31.8 jit_solution(5947822495948194951)
XLA Ops:
  0.0 1.2 %bitcast_convert_fusion.moduli_in = f32[1,16]{1,0:T(1,128)} fusion(bf16[16]{0:T(256)(128)(2,1)} %param.7), kind=kLoop, calls=%fused_computation | loop fusion | flops 16 | bytes 96 | tf_op jit(solution)/shard_map/reshape | solution.py:368
  1.2 29.3 %shard_map.46 = f32[16,256]{1,0:T(8,128)} custom-call(bf16[16,1024,256]{2,1,0:T(8,128)(2,1)} %bitcast.4, s32[16,1024]{1,0:T(8,128)} %material_in.1, s32[1,4]{1,0:T(1,128)} %occupancy_in.1, f32[1,16]{1,0:T(1,128)} %bitcast_convert_fusion.moduli_in), custom_call_target="tpu_custom_call" | custom-call | flops 10737418240 | bytes 8388608 | tf_op jit(solution)/shard_map/pallas_call | solution.py:324
  30.4 1.3 %copy.6 = f32[16,256]{1,0:T(8,128)} copy(f32[16,256]{1,0:T(8,128)} %shard_map.46) | data formatting | bytes 32768

commit v3 on v2

--- a/solution.py
+++ b/solution.py
@@ -41,7 +41,7 @@
 def kernel(
     n, rows_y, rows_x, scale,
     snap, material_in, occupancy_in, moduli_in, out,
-    field, newest, pair, split, weights, weights_next, columns, total, share, mate, mine, arrived,
+    field, older, newest, around_first, split, weights, weights_next, columns, total, share, mate, mine, arrived,
     edge_out, edge_in, material, occupancy, moduli,
     load_sem, small_sem, plane_send, plane_recv, edge_send, edge_recv, share_send, share_recv,
     mate_send, mate_recv,
@@ -85,7 +85,7 @@
     classes = material[...]
     modulus = jnp.zeros((depth, plane), jnp.float32)
     for c in range(moduli.shape[1]):
-        modulus = jnp.where(classes == c, moduli[0:1, c : c + 1], modulus)
+        modulus = jnp.where(classes == c, moduli[0:1, c : c + 1].astype(jnp.float32), modulus)
     modulus = modulus * occupied
     edge_out[0, 0:1, :] = modulus[0:1]
     edge_out[0, 1:2, :] = occupied
@@ -111,6 +111,30 @@
             device_id={"bricks": below},
         )
 
+    fill_weights(weights, occupied, rows_y, rows_x)
+    total[...] = jnp.zeros_like(total)
+
+    def chunks():
+        for start, first, last in windows(rows_y):
+            yield (
+                slice(first * rows_x, last * rows_x),
+                slice(start * rows_x, (start + 8) * rows_x),
+            )
+
+    def convolve(table, z, rows, window):
+        return jnp.dot(
+            table[rows, :], field[z, window, :], preferred_element_type=jnp.float32
+        )
+
+    loads[0].wait()
+    loads[1].wait()
+    for rows, window in chunks():
+        plane_0 = convolve(weights, 0, rows, window)
+        plane_1 = convolve(weights, 1, rows, window)
+        older[rows, :] = plane_0
+        newest[rows, :] = plane_1
+        around_first[rows, :] = 2.0 * plane_0 + plane_1
+
     pl.semaphore_wait(barrier, n // 2 + 1)
 
     @pl.when(me > 0)
@@ -131,59 +155,39 @@
     def _():
         edge_in[1] = jnp.zeros(edge_in.shape[1:], jnp.float32)
 
-    fill_weights(weights, occupied, rows_y, rows_x)
-    total[...] = jnp.zeros_like(total)
-    split[1] = jnp.zeros(split.shape[1:], jnp.bfloat16)
-    loads[0].wait()
-    for start, first, last in windows(rows_y):
-        rows = slice(first * rows_x, last * rows_x)
-        fresh = jnp.dot(
-            weights[rows, :],
-            field[0, start * rows_x : (start + 8) * rows_x, :],
-            preferred_element_type=jnp.float32,
-        )
-        newest[rows, :] = fresh
-        pair[rows, :] = fresh
-
-    @pl.when(me < n - 1)
-    def _():
-        edge_copy(0).wait_recv()
-
-    @pl.when(me > 0)
-    def _():
-        edge_copy(1).wait_recv()
-
-    fill_weights(weights_next, edge_in[0, 1:2, :], rows_y, rows_x)
-
-    moduli_all = jnp.concatenate(
-        [modulus, edge_in[0, 0:1, :], edge_in[1, 0:1, :], jnp.zeros((6, plane), jnp.float32)], 0
-    )
-    summed = moduli_all
-    for at, count, step in ((at_x, rows_x, 1), (at_y, rows_y, rows_x)):
-        lower = jnp.where(at > 0, pltpu.roll(summed, step, 1), 0.0)
-        upper = jnp.where(at < count - 1, pltpu.roll(summed, plane - step, 1), 0.0)
-        summed = lower + upper + 2.0 * summed
-    around = (
-        jnp.concatenate([summed[depth + 1 : depth + 2], summed[: depth - 1]], 0)
-        + 2.0 * summed[:depth]
-        + summed[1 : depth + 1]
-    )
-    diagonal = (4.0 * modulus + 0.0625 * around) * occupied
-    diagonal_high = diagonal.astype(jnp.bfloat16).astype(jnp.float32)
-    gap = jnp.zeros((32 - depth, plane), jnp.float32)
-    stack = jnp.concatenate(
-        [
-            0.125 * moduli_all,
-            jnp.zeros((8, plane), jnp.float32),
-            diagonal_high,
-            gap,
-            diagonal - diagonal_high,
-            gap,
-            jnp.zeros((32, plane), jnp.float32),
-        ],
-        0,
-    )
-    columns[...] = stack.T.astype(jnp.bfloat16)
+    def fill_columns(next_plane, last_plane):
+        moduli_all = jnp.concatenate(
+            [modulus, next_plane, last_plane, jnp.zeros((6, plane), jnp.float32)], 0
+        )
+        summed = moduli_all
+        for at, count, step in ((at_x, rows_x, 1), (at_y, rows_y, rows_x)):
+            lower = jnp.where(at > 0, pltpu.roll(summed, step, 1), 0.0)
+            upper = jnp.where(at < count - 1, pltpu.roll(summed, plane - step, 1), 0.0)
+            summed = lower + upper + 2.0 * summed
+        around = (
+            jnp.concatenate([summed[depth + 1 : depth + 2], summed[: depth - 1]], 0)
+            + 2.0 * summed[:depth]
+            + summed[1 : depth + 1]
+        )
+        diagonal = (4.0 * modulus + 0.0625 * around) * occupied
+        diagonal_high = diagonal.astype(jnp.bfloat16).astype(jnp.float32)
+        gap = jnp.zeros((32 - depth, plane), jnp.float32)
+        stack = jnp.concatenate(
+            [
+                0.125 * moduli_all,
+                jnp.zeros((8, plane), jnp.float32),
+                diagonal_high,
+                gap,
+                diagonal - diagonal_high,
+                gap,
+                jnp.zeros((32, plane), jnp.float32),
+            ],
+            0,
+        )
+        columns[...] = stack.T.astype(jnp.bfloat16)
+
+    nothing = jnp.zeros((1, plane), jnp.float32)
+    fill_columns(nothing, nothing)
 
     def picker(z):
         row = lax.broadcasted_iota(jnp.int32, (128, 256), 0)
@@ -192,71 +196,101 @@
         is_diagonal = (col >= 128) & ((row == z + 32) | (row == z + 64))
         return jnp.where(is_modulus | is_diagonal, 1.0, 0.0).astype(jnp.bfloat16)
 
-    def put(slot, rows, part, value):
+    def put(slot, place, rows, part, value):
+        rows = slice(place * plane + rows.start, place * plane + rows.stop)
         high = value.astype(jnp.bfloat16)
         split[slot, rows, part * 128 : (part + 1) * 128] = high
         split[slot, rows, width + part * 128 : width + (part + 1) * 128] = (
             value - high.astype(jnp.float32)
         ).astype(jnp.bfloat16)
 
-    def add_gram(z, slot):
+    def parts():
+        for part in range(width // 128):
+            yield part, slice(part * 128, (part + 1) * 128)
+
+    def spread_over(pick, rows):
+        both = jnp.dot(columns[rows, :], pick, preferred_element_type=jnp.float32)
+        return both[:, :128], both[:, 128:]
+
+    def add_gram(z, slot, planes=2):
         total[...] += lax.dot_general(
-            field[z], split[slot], TRANSPOSED, preferred_element_type=jnp.float32
-        )
-
-    def one_plane(z, slot, table, last_plane=False):
-        pick = picker(z)
-        for index, (start, first, last) in enumerate(windows(rows_y)):
-            rows = slice(first * rows_x, last * rows_x)
-            fresh = jnp.dot(
-                table[rows, :],
-                field[z + 1, start * rows_x : (start + 8) * rows_x, :],
-                preferred_element_type=jnp.float32,
-            )
-            spread = jnp.dot(columns[rows, :], pick, preferred_element_type=jnp.float32)
-            for part in range(width // 128):
-                lanes = slice(part * 128, (part + 1) * 128)
-                later = newest[rows, lanes] + fresh[:, lanes]
-                around = pair[rows, lanes] + later
-                if not last_plane:
-                    newest[rows, lanes] = fresh[:, lanes]
-                    pair[rows, lanes] = later
-                value = (
-                    spread[:, 128:] * field[z, rows, lanes].astype(jnp.float32)
-                    - spread[:, :128] * around
-                )
-                put(slot, rows, part, value)
-            if index == 2:
-                add_gram(jnp.maximum(z - 1, 0), 1 - slot)
+            field[pl.ds(z, planes)].reshape(planes * plane, width),
+            split[slot, : planes * plane, :],
+            TRANSPOSED,
+            preferred_element_type=jnp.float32,
+        )
 
     def wait_plane(z):
         pltpu.make_async_copy(snap.at[z], field.at[z], load_sem.at[z]).wait()
 
+    def two_planes(z, slot, gram_before=True):
+        pick_a, pick_b = picker(z), picker(z + 1)
+        for index, (rows, window) in enumerate(chunks()):
+            fresh_a = convolve(weights, z + 1, rows, window)
+            fresh_b = convolve(weights, z + 2, rows, window)
+            m_a, d_a = spread_over(pick_a, rows)
+            m_b, d_b = spread_over(pick_b, rows)
+            for part, lanes in parts():
+                before, now = older[rows, lanes], newest[rows, lanes]
+                first, second = fresh_a[:, lanes], fresh_b[:, lanes]
+                older[rows, lanes] = first
+                newest[rows, lanes] = second
+                middle = now + first
+                around_a = (before + now) + middle
+                around_b = middle + (first + second)
+                here_a = field[z, rows, lanes].astype(jnp.float32)
+                here_b = field[z + 1, rows, lanes].astype(jnp.float32)
+                put(slot, 0, rows, part, d_a * here_a - m_a * around_a)
+                put(slot, 1, rows, part, d_b * here_b - m_b * around_b)
+            if index == 2 and gram_before:
+                add_gram(z - 2, 1 - slot)
+
+    wait_plane(2)
+    wait_plane(3)
+    two_planes(1, 0, gram_before=False)
+
     def step(i, carry):
-        wait_plane(2 * i + 1)
-        wait_plane(2 * i + 2)
-        one_plane(2 * i, 0, weights)
-        one_plane(2 * i + 1, 1, weights)
+        for ahead in range(6, 10):
+            wait_plane(4 * i + ahead - 2)
+        two_planes(4 * i + 3, 1)
+        two_planes(4 * i + 5, 0)
         return carry
 
-    lax.fori_loop(0, depth // 2 - 1, step, 0)
-    wait_plane(depth - 1)
-    one_plane(depth - 2, 0, weights)
+    lax.fori_loop(0, (depth - 4) // 4, step, 0)
 
     @pl.when(me < n - 1)
     def _():
+        edge_copy(0).wait_recv()
         plane_copy().wait_recv()
 
-    one_plane(depth - 1, 1, weights_next, last_plane=True)
-    pick = picker(depth)
-    for start, first, last in windows(rows_y):
-        rows = slice(first * rows_x, last * rows_x)
-        spread = jnp.dot(columns[rows, :], pick, preferred_element_type=jnp.float32)
-        for part in range(width // 128):
-            lanes = slice(part * 128, (part + 1) * 128)
-            put(0, rows, part, -spread[:, :128] * newest[rows, lanes])
-    add_gram(depth - 1, 1)
-    add_gram(depth, 0)
+    @pl.when(me > 0)
+    def _():
+        edge_copy(1).wait_recv()
+
+    fill_weights(weights_next, edge_in[0, 1:2, :], rows_y, rows_x)
+    fill_columns(edge_in[0, 0:1, :], edge_in[1, 0:1, :])
+    pick_a, pick_b = picker(depth - 1), picker(depth)
+    for index, (rows, window) in enumerate(chunks()):
+        fresh = convolve(weights_next, depth, rows, window)
+        m_a, d_a = spread_over(pick_a, rows)
+        m_b, _ = spread_over(pick_b, rows)
+        for part, lanes in parts():
+            now = newest[rows, lanes]
+            around = older[rows, lanes] + 2.0 * now + fresh[:, lanes]
+            here = field[depth - 1, rows, lanes].astype(jnp.float32)
+            put(1, 0, rows, part, d_a * here - m_a * around)
+            put(1, 1, rows, part, -m_b * now)
+        if index == 2:
+            add_gram(depth - 3, 0)
+    pick = picker(0)
+    for index, (rows, window) in enumerate(chunks()):
+        m, d = spread_over(pick, rows)
+        for part, lanes in parts():
+            here = field[0, rows, lanes].astype(jnp.float32)
+            put(0, 0, rows, part, d * here - m * around_first[rows, lanes])
+        if index == 2:
+            add_gram(depth - 1, 1)
+    add_gram(0, 0, planes=1)
 
     half = total[:, :width] + total[:, width:]
     gram = (half + half.T) * scale
@@ -330,7 +364,8 @@
             pltpu.VMEM((depth + 1, plane, width), bf16),
             pltpu.VMEM((plane, width), f32),
             pltpu.VMEM((plane, width), f32),
-            pltpu.VMEM((2, plane, 2 * width), bf16),
+            pltpu.VMEM((plane, width), f32),
+            pltpu.VMEM((2, 2 * plane, 2 * width), bf16),
             pltpu.VMEM((plane, 8 * rows_x), bf16),
             pltpu.VMEM((plane, 8 * rows_x), bf16),
             pltpu.VMEM((plane, 128), bf16),
@@ -343,7 +378,7 @@
             pltpu.VMEM((2, 8, plane), f32),
             pltpu.VMEM(material.shape, jnp.int32),
             pltpu.VMEM(occupancy.shape, jnp.int32),
-            pltpu.VMEM((1, moduli.shape[0]), f32),
+            pltpu.VMEM((1, moduli.shape[0]), bf16),
             pltpu.SemaphoreType.DMA((depth,)),
             pltpu.SemaphoreType.DMA((3,)),
             pltpu.SemaphoreType.DMA,
@@ -365,7 +400,7 @@
         snapshots.reshape(depth, plane, width),
         material,
         occupancy,
-        moduli.astype(f32).reshape(1, -1),
+        moduli.reshape(1, -1),
     )
 
 

time: 32 us -> 29.5 us (0.922)
  Pallas kernels: 29.3 us -> 27.9 us
  other arithmetic: 1.17 us -> 0 us
    pallas_call x1, Pallas kernels: 29.3 us -> 27.9 us  [local(): pl.pallas_call(functools.partial(kernel, n, rows_y, rows_x, 1.0 / (depth...]
    reshape x1 -> x0, other arithmetic: 1.17 us -> none  [local(): moduli.astype(f32).reshape(1, -1)]
where the time goes in v3:
time: 29.5 us; the launch traced here: 29.2 us
  Pallas kernels  27.9 us (95%)
  local copies, waits for them, and re-layouts  1.32 us (4%)
    pallas_call x1, Pallas kernels, local(): pl.pallas_call(functools.partial(kernel, n, rows_y, rows_x, 1.0 / (depth...  27.9 us
    unnamed x1, local copies, waits for them, and re-layouts  1.32 us

profile of v3, /device:TPU:0, one launch (start us, length us, event | category | flops | bytes accessed | tf_op | source)
XLA Modules:
  0.0 29.2 jit_solution(2931295548752557021)
XLA Ops:
  0.0 27.9 %shard_map.46 = f32[16,256]{1,0:T(8,128)} custom-call(bf16[16,1024,256]{2,1,0:T(8,128)(2,1)} %bitcast.2, s32[16,1024]{1,0:T(8,128)} %material_in.1, s32[1,4]{1,0:T(1,128)} %occupancy_in.1, bf16[1,16]{1,0:T(2,128)(2,1)} %bitcast.3), custom_call_target="tpu_custom_call" | custom-call | flops 10737418240 | bytes 8388608 | tf_op jit(solution)/shard_map/pallas_call | solution.py:358
  27.9 1.3 %copy.6 = f32[16,256]{1,0:T(8,128)} copy(f32[16,256]{1,0:T(8,128)} %shard_map.46) | data formatting | bytes 32768

commit v4 on v3

--- a/solution.py
+++ b/solution.py
@@ -155,7 +155,7 @@
     def _():
         edge_in[1] = jnp.zeros(edge_in.shape[1:], jnp.float32)
 
-    def fill_columns(next_plane, last_plane):
+    def fill_columns(next_plane, last_plane, copies):
         moduli_all = jnp.concatenate(
             [modulus, next_plane, last_plane, jnp.zeros((6, plane), jnp.float32)], 0
         )
@@ -170,31 +170,22 @@
             + summed[1 : depth + 1]
         )
         diagonal = (4.0 * modulus + 0.0625 * around) * occupied
-        diagonal_high = diagonal.astype(jnp.bfloat16).astype(jnp.float32)
-        gap = jnp.zeros((32 - depth, plane), jnp.float32)
         stack = jnp.concatenate(
             [
                 0.125 * moduli_all,
                 jnp.zeros((8, plane), jnp.float32),
-                diagonal_high,
-                gap,
-                diagonal - diagonal_high,
-                gap,
-                jnp.zeros((32, plane), jnp.float32),
+                diagonal,
+                jnp.zeros((96 - depth, plane), jnp.float32),
             ],
             0,
         )
-        columns[...] = stack.T.astype(jnp.bfloat16)
+        upright = stack.T
+        columns[0] = upright
+        for copy in range(1, copies):
+            columns[copy] = pltpu.roll(upright, 128 - 4 * copy, 1)
 
     nothing = jnp.zeros((1, plane), jnp.float32)
-    fill_columns(nothing, nothing)
-
-    def picker(z):
-        row = lax.broadcasted_iota(jnp.int32, (128, 256), 0)
-        col = lax.broadcasted_iota(jnp.int32, (128, 256), 1)
-        is_modulus = (col < 128) & (row == z)
-        is_diagonal = (col >= 128) & ((row == z + 32) | (row == z + 64))
-        return jnp.where(is_modulus | is_diagonal, 1.0, 0.0).astype(jnp.bfloat16)
+    fill_columns(nothing, nothing, columns.shape[0])
 
     def put(slot, place, rows, part, value):
         rows = slice(place * plane + rows.start, place * plane + rows.stop)
@@ -208,9 +199,11 @@
         for part in range(width // 128):
             yield part, slice(part * 128, (part + 1) * 128)
 
-    def spread_over(pick, rows):
-        both = jnp.dot(columns[rows, :], pick, preferred_element_type=jnp.float32)
-        return both[:, :128], both[:, 128:]
+    def spread_over(copy, lane, rows):
+        shape = (rows.stop - rows.start, 128)
+        m = columns[copy, rows, lane : lane + 1]
+        d = columns[copy, rows, lane + 32 : lane + 33]
+        return jnp.broadcast_to(m, shape), jnp.broadcast_to(d, shape)
 
     def add_gram(z, slot, planes=2):
         total[...] += lax.dot_general(
@@ -223,13 +216,12 @@
     def wait_plane(z):
         pltpu.make_async_copy(snap.at[z], field.at[z], load_sem.at[z]).wait()
 
-    def two_planes(z, slot, gram_before=True):
-        pick_a, pick_b = picker(z), picker(z + 1)
+    def two_planes(z, slot, copy, lane, gram_before=True):
         for index, (rows, window) in enumerate(chunks()):
             fresh_a = convolve(weights, z + 1, rows, window)
             fresh_b = convolve(weights, z + 2, rows, window)
-            m_a, d_a = spread_over(pick_a, rows)
-            m_b, d_b = spread_over(pick_b, rows)
+            m_a, d_a = spread_over(copy, lane, rows)
+            m_b, d_b = spread_over(copy, lane + 1, rows)
             for part, lanes in parts():
                 before, now = older[rows, lanes], newest[rows, lanes]
                 first, second = fresh_a[:, lanes], fresh_b[:, lanes]
@@ -247,13 +239,13 @@
 
     wait_plane(2)
     wait_plane(3)
-    two_planes(1, 0, gram_before=False)
+    two_planes(1, 0, 0, 1, gram_before=False)
 
     def step(i, carry):
         for ahead in range(6, 10):
             wait_plane(4 * i + ahead - 2)
-        two_planes(4 * i + 3, 1)
-        two_planes(4 * i + 5, 0)
+        two_planes(4 * i + 3, 1, i, 3)
+        two_planes(4 * i + 5, 0, i, 5)
         return carry
 
     lax.fori_loop(0, (depth - 4) // 4, step, 0)
@@ -268,12 +260,11 @@
         edge_copy(1).wait_recv()
 
     fill_weights(weights_next, edge_in[0, 1:2, :], rows_y, rows_x)
-    fill_columns(edge_in[0, 0:1, :], edge_in[1, 0:1, :])
-    pick_a, pick_b = picker(depth - 1), picker(depth)
+    fill_columns(edge_in[0, 0:1, :], edge_in[1, 0:1, :], 1)
     for index, (rows, window) in enumerate(chunks()):
         fresh = convolve(weights_next, depth, rows, window)
-        m_a, d_a = spread_over(pick_a, rows)
-        m_b, _ = spread_over(pick_b, rows)
+        m_a, d_a = spread_over(0, depth - 1, rows)
+        m_b, _ = spread_over(0, depth, rows)
         for part, lanes in parts():
             now = newest[rows, lanes]
             around = older[rows, lanes] + 2.0 * now + fresh[:, lanes]
@@ -282,9 +273,8 @@
             put(1, 1, rows, part, -m_b * now)
         if index == 2:
             add_gram(depth - 3, 0)
-    pick = picker(0)
     for index, (rows, window) in enumerate(chunks()):
-        m, d = spread_over(pick, rows)
+        m, d = spread_over(0, 0, rows)
         for part, lanes in parts():
             here = field[0, rows, lanes].astype(jnp.float32)
             put(0, 0, rows, part, d * here - m * around_first[rows, lanes])
@@ -368,7 +358,7 @@
             pltpu.VMEM((2, 2 * plane, 2 * width), bf16),
             pltpu.VMEM((plane, 8 * rows_x), bf16),
             pltpu.VMEM((plane, 8 * rows_x), bf16),
-            pltpu.VMEM((plane, 128), bf16),
+            pltpu.VMEM(((depth - 4) // 4, plane, 128), f32),
             pltpu.VMEM((width, 2 * width), f32),
             pltpu.VMEM((2, n // 2, own, width), f32),
             pltpu.VMEM((n // 2, own, width), f32),

time: 29.5 us -> 29 us (0.983)
  Pallas kernels: 27.9 us -> 27.4 us
    pallas_call x1, Pallas kernels: 27.9 us -> 27.4 us  [local(): pl.pallas_call(functools.partial(kernel, n, rows_y, rows_x, 1.0 / (depth...]
where the time goes in v4:
time: 29 us; the launch traced here: 28.7 us
  Pallas kernels  27.4 us (94%)
  local copies, waits for them, and re-layouts  1.32 us (5%)
    pallas_call x1, Pallas kernels, local(): pl.pallas_call(functools.partial(kernel, n, rows_y, rows_x, 1.0 / (depth...  27.4 us
    unnamed x1, local copies, waits for them, and re-layouts  1.32 us

profile of v4, /device:TPU:0, one launch (start us, length us, event | category | flops | bytes accessed | tf_op | source)
XLA Modules:
  0.0 28.7 jit_solution(1502964222837984258)
XLA Ops:
  0.0 27.4 %shard_map.46 = f32[16,256]{1,0:T(8,128)} custom-call(bf16[16,1024,256]{2,1,0:T(8,128)(2,1)} %bitcast.2, s32[16,1024]{1,0:T(8,128)} %material_in.1, s32[1,4]{1,0:T(1,128)} %occupancy_in.1, bf16[1,16]{1,0:T(2,128)(2,1)} %bitcast.3), custom_call_target="tpu_custom_call" | custom-call | flops 10737418240 | bytes 8388608 | tf_op jit(solution)/shard_map/pallas_call | solution.py:348
  27.4 1.3 %copy.6 = f32[16,256]{1,0:T(8,128)} copy(f32[16,256]{1,0:T(8,128)} %shard_map.46) | data formatting | bytes 32768
